TPU v7x, 32 devices: a whole 2x2x4 slice. The times are simulated.
32 devices in a mesh: gx: 16 (over z, y, x), gy: 2 (over core).
Axes of the slice: x: 2, y: 2, z: 4, core: 2. Of those that a mesh axis runs over, the one named last changes fastest.
Arguments:
- orbitals: bfloat16 [112, 14, 8, 256], P('gx', 'gy'), may hold values from -6 to 6
- cell_ham: bfloat16 [16, 2, 512, 512], P('gx', 'gy'), may hold values from -0.4 to 2.4, as said below
- proj_vals: bfloat16 [16, 2, 32, 512], P('gx', 'gy'), may hold values from -0.25 to 0.25
- proj_ids: int32 [16, 2, 32], P('gx', 'gy'), may hold values from 0 to 63
- coupling: float32 [16, 64], P('gx'), may hold values from 0.5 to 2
Outputs:
- filtered: float32 [112, 14, 8, 256], P('gx', 'gy')
Inputs may be any that keep to these rules, and one draw needn't show every extreme that they name: `cell_ham`: each cell matrix is symmetric.
All inputs are finite; a program needn't handle non-finite values.
Results may differ from a plain program's by a relative error of at most 0.0054.
Values may be sent and summed in bfloat16 or wider, within the bound.
A program may use at most 64 MiB of HBM per device.

v0:
```python
import jax
import jax.numpy as jnp
from jax import lax
from jax.sharding import PartitionSpec as P

ORDER = 7
NODES = 512
DEGREE = 4
SLOTS = 32
PROJ_GROUP = 64


center = 5.0
half_width = 9.0


def from_behind(block, axis, distance):
    devices = range(lax.axis_size(axis))
    route = [((i - distance) % len(devices), i) for i in devices]
    return lax.ppermute(block, axis, route)


def gather_cells(extended, cells_x, cells_y):
    points = ORDER + 1
    trailing = extended.shape[1:]
    row_part = jnp.concatenate(
        [
            extended[: ORDER * cells_x].reshape((cells_x, ORDER) + trailing),
            extended[ORDER::ORDER][:, None],
        ],
        axis=1,
    )
    columns = jnp.concatenate(
        [
            row_part[:, :, : ORDER * cells_y].reshape(
                (cells_x, points, cells_y, ORDER) + trailing[1:]
            ),
            row_part[:, :, ORDER::ORDER][:, :, :, None],
        ],
        axis=3,
    )
    return columns.transpose(0, 2, 1, 3, 4, 5).reshape(cells_x * cells_y, NODES, trailing[-1])


def join_second(values, cells_y):
    leading = values.shape[:2]
    trailing = values.shape[4:]
    lower = values[:, :, :, :ORDER].reshape(leading + (ORDER * cells_y,) + trailing)
    upper = jnp.pad(
        values[:, :, :, ORDER:], ((0, 0), (0, 0), (0, 0), (0, ORDER - 1), (0, 0), (0, 0))
    ).reshape(leading + (ORDER * cells_y,) + trailing)
    no_pad = ((0, 0), (0, 0))
    return (
        jnp.pad(lower, no_pad + ((0, 1),) + no_pad)
        + jnp.pad(upper, no_pad + ((ORDER, 0),) + no_pad)[:, :, : ORDER * cells_y + 1]
    )


def join_first(joined, cells_x):
    trailing = joined.shape[2:]
    lower = joined[:, :ORDER].reshape((ORDER * cells_x,) + trailing)
    upper = jnp.pad(joined[:, ORDER:], ((0, 0), (0, ORDER - 1), (0, 0), (0, 0), (0, 0))).reshape(
        (ORDER * cells_x,) + trailing
    )
    no_pad = ((0, 0), (0, 0), (0, 0))
    return (
        jnp.pad(lower, ((0, 1),) + no_pad)
        + jnp.pad(upper, ((ORDER, 0),) + no_pad)[: ORDER * cells_x + 1]
    )


def cell_terms(extended, matrices, proj_rows, onehot, strength, cells_x, cells_y, reduce_sum):
    points = ORDER + 1
    cell_vals = gather_cells(extended, cells_x, cells_y)
    width = cell_vals.shape[-1]
    coefficient = jnp.einsum(
        "ksn,kno->kso", proj_rows, cell_vals, preferred_element_type=jnp.float32
    )
    local_sum = jnp.einsum("ksp,kso->po", onehot, coefficient, precision=lax.Precision.HIGHEST)
    totals = reduce_sum(local_sum)
    weights = strength[:, None] * totals
    per_slot = jnp.einsum("ksp,po->kso", onehot, weights, precision=lax.Precision.HIGHEST).astype(
        jnp.bfloat16
    )
    product = jnp.einsum("knm,kmo->kno", matrices, cell_vals, preferred_element_type=jnp.float32)
    product = product + jnp.einsum(
        "ksn,kso->kno", proj_rows, per_slot, preferred_element_type=jnp.float32
    )
    values = product.reshape(cells_x, cells_y, points, points, points, width).transpose(
        0, 2, 1, 3, 4, 5
    )
    return join_first(join_second(values, cells_y), cells_x)


def run_filter(start_field, apply_field):
    earlier = start_field.astype(jnp.float32)
    current = (apply_field(start_field) - center * earlier) / half_width
    for repeat in range(DEGREE - 1):
        image = apply_field(current.astype(jnp.bfloat16))
        following = 2.0 * (image - center * current) / half_width - earlier
        earlier, current = (current, following)
    return current


def per_device(orbitals, cell_ham, proj_vals, proj_ids, coupling):
    cells_x = cell_ham.shape[0]
    cells_y = cell_ham.shape[1]
    matrices = cell_ham.reshape(cells_x * cells_y, NODES, NODES)
    proj_rows = proj_vals.reshape(cells_x * cells_y, SLOTS, NODES)
    slot_ids = proj_ids.reshape(cells_x * cells_y, SLOTS)
    onehot = (slot_ids[:, :, None] == jnp.arange(PROJ_GROUP, dtype=jnp.int32)).astype(jnp.float32)
    strength = coupling[0]

    def reduce_sum(local_sum):
        return lax.psum(local_sum, "gy")

    def assemble_terms(extended):
        return cell_terms(
            extended, matrices, proj_rows, onehot, strength, cells_x, cells_y, reduce_sum
        )

    def apply_owned(field_in):
        upper = from_behind(field_in[:1], "gx", -1)
        extended = jnp.concatenate([field_in, upper], axis=0)
        beside = from_behind(extended[:, :1], "gy", -1)
        extended = jnp.concatenate([extended, beside], axis=1)
        summed = assemble_terms(extended)
        carried = from_behind(summed[:, -1:], "gy", 1)
        summed = summed[:, :-1].at[:, :1].add(carried)
        carried = from_behind(summed[-1:], "gx", 1)
        return summed[:-1].at[:1].add(carried)

    return run_filter(orbitals, apply_owned)


def solution(mesh):
    placed = (
        P("gx", "gy", None, None),
        P("gx", "gy", None, None),
        P("gx", "gy", None, None),
        P("gx", "gy", None),
        P("gx", None),
    )
    return jax.shard_map(
        per_device, mesh=mesh, in_specs=placed, out_specs=P("gx", "gy", None, None), check_vma=False
    )
```

profile of v0, /device:TPU:0, one launch (start us, length us, event | category | flops | bytes accessed | tf_op | source)
XLA Modules:
  0.0 168.1 jit_solution(6171479123098988289)
XLA Ops:
  6.5 0.8 slice.440
  7.3 6.9 %collective-permute-start = (bf16[1,7,8,256]{3,2,1,0:T(8,128)(2,1)S(1)}, bf16[1,7,8,256]{3,2,1,0:T(8,128)(2,1)S(1)}, u32[]{:S(2)}, u32[]{:S(2)}) collective-permute-start(bf16[1,7,8,256]{3,2,1,0:T(8,128)(2,1)S(1)} %slice.440), channel_id=1, source_target_pairs={{2,0},{4,2},{6,4},{8,6},{10,8},{12,10},{14,12},{16,14},{18,16},{20... | collective-permute-start | bytes 86024 | tf_op jit(solution)/shard_map/ppermute | solution.py:20
  14.3 0.9 constant_dynamic-update-slice_fusion.1
  15.2 0.6 collective-permute-done
  15.9 1.2 collective-permute-done.1
  17.2 0.7 copy-done.2
  17.9 0.3 fusion.58
  18.2 0.6 copy-done.3
  18.8 0.9 fusion.71
  19.8 0.3 fusion.18
  20.2 19.2 %all-reduce.29.cloned.1.call-done = f32[64,256]{1,0:T(8,128)} async-done(((f32[64,256]{1,0:T(8,128)}), f32[64,256]{1,0:T(8,128)}) %all-reduce.29.cloned.1.call-update) | async-done | bytes 65552 | tf_op jit(solution)/shard_map/psum | solution.py:115
  39.4 1.1 convolution_convert_fusion.3
  40.5 0.3 fusion.3
  40.7 0.2 copy.19
  41.2 0.3 collective-permute-start.2
  41.5 1.0 collective-permute-done.2
  42.5 1.8 %collective-permute-start.3 = (f32[1,7,8,256]{3,2,1,0:T(8,128)S(1)}, f32[1,7,8,256]{3,2,1,0:T(8,128)S(1)}, u32[]{:S(2)}, u32[]{:S(2)}) collective-permute-start(f32[1,7,8,256]{3,2,1,0:T(8,128)S(1)} %slice.526), channel_id=1, source_target_pairs={{30,0},{0,2},{2,4},{4,6},{6,8},{8,10},{10,12},{12,14},{14,16},{16,... | collective-permute-start | bytes 172040 | tf_op jit(solution)/shard_map/ppermute | solution.py:20
  44.4 6.0 %collective-permute-done.3 = f32[1,7,8,256]{3,2,1,0:T(8,128)S(1)} collective-permute-done((f32[1,7,8,256]{3,2,1,0:T(8,128)S(1)}, f32[1,7,8,256]{3,2,1,0:T(8,128)S(1)}, u32[]{:S(2)}, u32[]{:S(2)}) %collective-permute-start.3) | collective-permute-done | bytes 57376 | tf_op jit(solution)/shard_map/ppermute | solution.py:20
  50.4 0.1 multiply_convert_fusion
  50.5 1.9 %collective-permute-start.4 = (bf16[1,7,8,256]{3,2,1,0:T(8,128)(2,1)S(1)}, bf16[1,7,8,256]{3,2,1,0:T(8,128)(2,1)S(1)}, u32[]{:S(2)}, u32[]{:S(2)}) collective-permute-start(bf16[1,7,8,256]{3,2,1,0:T(8,128)(2,1)S(1)} %slice.527), channel_id=1, source_target_pairs={{2,0},{4,2},{6,4},{8,6},{10,8},{12,10},{14,12},{16,14},{18,16},{20... | collective-permute-start | bytes 86024 | tf_op jit(solution)/shard_map/ppermute | solution.py:20
  52.3 2.1 %collective-permute-done.4 = bf16[1,7,8,256]{3,2,1,0:T(8,128)(2,1)S(1)} collective-permute-done((bf16[1,7,8,256]{3,2,1,0:T(8,128)(2,1)S(1)}, bf16[1,7,8,256]{3,2,1,0:T(8,128)(2,1)S(1)}, u32[]{:S(2)}, u32[]{:S(2)}) %collective-permute-start.4) | collective-permute-done | bytes 28704 | tf_op jit(solution)/shard_map/ppermute | solution.py:20
  54.4 1.2 collective-permute-done.5
  55.8 0.3 fusion.55
  56.1 0.9 fusion.69
  57.1 0.3 fusion.16
  57.4 18.6 %all-reduce.31.cloned.1.call-done = f32[64,256]{1,0:T(8,128)} async-done(((f32[64,256]{1,0:T(8,128)}), f32[64,256]{1,0:T(8,128)}) %all-reduce.31.cloned.1.call-update) | async-done | bytes 65552 | tf_op jit(solution)/shard_map/psum | solution.py:115
  76.1 1.1 convolution_convert_fusion.2
  77.1 0.2 fusion.2
  77.4 0.2 copy.21
  77.9 0.3 collective-permute-start.6
  78.2 1.0 collective-permute-done.6
  79.2 1.8 %collective-permute-start.7 = (f32[1,7,8,256]{3,2,1,0:T(8,128)S(1)}, f32[1,7,8,256]{3,2,1,0:T(8,128)S(1)}, u32[]{:S(2)}, u32[]{:S(2)}) collective-permute-start(f32[1,7,8,256]{3,2,1,0:T(8,128)S(1)} %slice.540), channel_id=1, source_target_pairs={{30,0},{0,2},{2,4},{4,6},{6,8},{8,10},{10,12},{12,14},{14,16},{16,... | collective-permute-start | bytes 172040 | tf_op jit(solution)/shard_map/ppermute | solution.py:20
  81.0 6.0 %collective-permute-done.7 = f32[1,7,8,256]{3,2,1,0:T(8,128)S(1)} collective-permute-done((f32[1,7,8,256]{3,2,1,0:T(8,128)S(1)}, f32[1,7,8,256]{3,2,1,0:T(8,128)S(1)}, u32[]{:S(2)}, u32[]{:S(2)}) %collective-permute-start.7) | collective-permute-done | bytes 57376 | tf_op jit(solution)/shard_map/ppermute | solution.py:20
  87.1 0.1 fusion.82
  87.2 1.9 %collective-permute-start.8 = (bf16[1,7,8,256]{3,2,1,0:T(8,128)(2,1)S(1)}, bf16[1,7,8,256]{3,2,1,0:T(8,128)(2,1)S(1)}, u32[]{:S(2)}, u32[]{:S(2)}) collective-permute-start(bf16[1,7,8,256]{3,2,1,0:T(8,128)(2,1)S(1)} %slice.541), channel_id=1, source_target_pairs={{2,0},{4,2},{6,4},{8,6},{10,8},{12,10},{14,12},{16,14},{18,16},{20... | collective-permute-start | bytes 86024 | tf_op jit(solution)/shard_map/ppermute | solution.py:20
  89.0 2.1 %collective-permute-done.8 = bf16[1,7,8,256]{3,2,1,0:T(8,128)(2,1)S(1)} collective-permute-done((bf16[1,7,8,256]{3,2,1,0:T(8,128)(2,1)S(1)}, bf16[1,7,8,256]{3,2,1,0:T(8,128)(2,1)S(1)}, u32[]{:S(2)}, u32[]{:S(2)}) %collective-permute-start.8) | collective-permute-done | bytes 28704 | tf_op jit(solution)/shard_map/ppermute | solution.py:20
  91.1 1.2 collective-permute-done.9
  92.5 0.3 fusion.52
  92.8 0.9 fusion.67
  93.8 0.3 fusion.14
  94.1 18.6 %all-reduce.33.cloned.1.call-done = f32[64,256]{1,0:T(8,128)} async-done(((f32[64,256]{1,0:T(8,128)}), f32[64,256]{1,0:T(8,128)}) %all-reduce.33.cloned.1.call-update) | async-done | bytes 65552 | tf_op jit(solution)/shard_map/psum | solution.py:115
  112.8 1.1 convolution_convert_fusion.1
  113.8 0.3 fusion.1
  114.1 0.2 copy.23
  114.6 0.3 collective-permute-start.10
  114.9 1.0 collective-permute-done.10
  115.9 1.8 %collective-permute-start.11 = (f32[1,7,8,256]{3,2,1,0:T(8,128)S(1)}, f32[1,7,8,256]{3,2,1,0:T(8,128)S(1)}, u32[]{:S(2)}, u32[]{:S(2)}) collective-permute-start(f32[1,7,8,256]{3,2,1,0:T(8,128)S(1)} %slice.554), channel_id=1, source_target_pairs={{30,0},{0,2},{2,4},{4,6},{6,8},{8,10},{10,12},{12,14},{14,16},{16,... | collective-permute-start | bytes 172040 | tf_op jit(solution)/shard_map/ppermute | solution.py:20
  117.7 6.0 %collective-permute-done.11 = f32[1,7,8,256]{3,2,1,0:T(8,128)S(1)} collective-permute-done((f32[1,7,8,256]{3,2,1,0:T(8,128)S(1)}, f32[1,7,8,256]{3,2,1,0:T(8,128)S(1)}, u32[]{:S(2)}, u32[]{:S(2)}) %collective-permute-start.11) | collective-permute-done | bytes 57376 | tf_op jit(solution)/shard_map/ppermute | solution.py:20
  123.8 0.2 fusion.81
  124.0 1.9 %collective-permute-start.12 = (bf16[1,7,8,256]{3,2,1,0:T(8,128)(2,1)S(1)}, bf16[1,7,8,256]{3,2,1,0:T(8,128)(2,1)S(1)}, u32[]{:S(2)}, u32[]{:S(2)}) collective-permute-start(bf16[1,7,8,256]{3,2,1,0:T(8,128)(2,1)S(1)} %slice.555), channel_id=1, source_target_pairs={{2,0},{4,2},{6,4},{8,6},{10,8},{12,10},{14,12},{16,14},{18,16},{20... | collective-permute-start | bytes 86024 | tf_op jit(solution)/shard_map/ppermute | solution.py:20
  125.8 2.1 %collective-permute-done.12 = bf16[1,7,8,256]{3,2,1,0:T(8,128)(2,1)S(1)} collective-permute-done((bf16[1,7,8,256]{3,2,1,0:T(8,128)(2,1)S(1)}, bf16[1,7,8,256]{3,2,1,0:T(8,128)(2,1)S(1)}, u32[]{:S(2)}, u32[]{:S(2)}) %collective-permute-start.12) | collective-permute-done | bytes 28704 | tf_op jit(solution)/shard_map/ppermute | solution.py:20
  127.9 1.2 collective-permute-done.13
  129.3 0.3 fusion.49
  129.5 0.9 fusion.65
  130.5 0.3 fusion.12
  130.9 18.7 %all-reduce.35.cloned.1.call-done = f32[64,256]{1,0:T(8,128)} async-done(((f32[64,256]{1,0:T(8,128)}), f32[64,256]{1,0:T(8,128)}) %all-reduce.35.cloned.1.call-update) | async-done | bytes 65552 | tf_op jit(solution)/shard_map/psum | solution.py:115
  149.5 1.1 convolution_convert_fusion
  150.6 0.3 fusion
  150.9 0.2 copy.25
  151.4 0.3 collective-permute-start.14
  151.7 1.0 collective-permute-done.14
  152.7 1.8 %collective-permute-start.15 = (f32[1,7,8,256]{3,2,1,0:T(8,128)S(1)}, f32[1,7,8,256]{3,2,1,0:T(8,128)S(1)}, u32[]{:S(2)}, u32[]{:S(2)}) collective-permute-start(f32[1,7,8,256]{3,2,1,0:T(8,128)S(1)} %slice.568), channel_id=1, source_target_pairs={{30,0},{0,2},{2,4},{4,6},{6,8},{8,10},{10,12},{12,14},{14,16},{16,... | collective-permute-start | bytes 172040 | tf_op jit(solution)/shard_map/ppermute | solution.py:20
  154.5 6.0 %collective-permute-done.15 = f32[1,7,8,256]{3,2,1,0:T(8,128)S(1)} collective-permute-done((f32[1,7,8,256]{3,2,1,0:T(8,128)S(1)}, f32[1,7,8,256]{3,2,1,0:T(8,128)S(1)}, u32[]{:S(2)}, u32[]{:S(2)}) %collective-permute-start.15) | collective-permute-done | bytes 57376 | tf_op jit(solution)/shard_map/ppermute | solution.py:20
  160.6 1.0 multiply_subtract_fusion
  (106 shorter events, 1.9 us)
Async XLA Ops:
  6.5 13.3 %copy-start = (bf16[1,1,512,512]{3,2,1,0:T(8,128)(2,1)S(1)}, bf16[1,1,512,512]{3,2,1,0:T(8,128)(2,1)}, u32[]{:S(2)}) copy-start(bf16[1,1,512,512]{3,2,1,0:T(8,128)(2,1)} %param.22) | copy-start | bytes 1572868
  6.5 32.8 %all-reduce.29.cloned.1.call-start = ((), (), s32[]{:S(2)}) async-start(), calls=%async_computation | async-start | bytes 131072 | tf_op jit(solution)/shard_map/psum | solution.py:115
  7.3 8.5 %collective-permute-start = (bf16[1,7,8,256]{3,2,1,0:T(8,128)(2,1)S(1)}, bf16[1,7,8,256]{3,2,1,0:T(8,128)(2,1)S(1)}, u32[]{:S(2)}, u32[]{:S(2)}) collective-permute-start(bf16[1,7,8,256]{3,2,1,0:T(8,128)(2,1)S(1)} %slice.440), channel_id=1, source_target_pairs={{2,0},{4,2},{6,4},{8,6},{10,8},{12,10},{14,12},{16,14},{18,16},{20... | collective-permute-start | bytes 86024 | tf_op jit(solution)/shard_map/ppermute | solution.py:20
  15.8 1.2 collective-permute-start.1
  17.1 0.8 copy-start.2
  18.2 0.7 copy-start.3
  19.8 56.3 %all-reduce.31.cloned.1.call-start = ((), (), s32[]{:S(2)}) async-start(), calls=%async_computation.1 | async-start | bytes 131072 | tf_op jit(solution)/shard_map/psum | solution.py:115
  20.2 19.2 %copy-start.4 = (f32[1,64]{1,0:T(1,128)S(1)}, f32[1,64]{1,0:T(1,128)}, u32[]{:S(2)}) copy-start(f32[1,64]{1,0:T(1,128)} %param.25) | copy-start | bytes 772
  41.2 1.3 collective-permute-start.2
  42.5 7.8 %collective-permute-start.3 = (f32[1,7,8,256]{3,2,1,0:T(8,128)S(1)}, f32[1,7,8,256]{3,2,1,0:T(8,128)S(1)}, u32[]{:S(2)}, u32[]{:S(2)}) collective-permute-start(f32[1,7,8,256]{3,2,1,0:T(8,128)S(1)} %slice.526), channel_id=1, source_target_pairs={{30,0},{0,2},{2,4},{4,6},{6,8},{8,10},{10,12},{12,14},{14,16},{16,... | collective-permute-start | bytes 172040 | tf_op jit(solution)/shard_map/ppermute | solution.py:20
  44.3 6.1 %copy-start.1 = (bf16[7,7,8,256]{3,2,1,0:T(8,128)(2,1)S(1)}, bf16[7,7,8,256]{3,2,1,0:T(8,128)(2,1)}, u32[]{:S(2)}) copy-start(bf16[7,7,8,256]{3,2,1,0:T(8,128)(2,1)} %param.21) | copy-start | bytes 602116
  50.5 3.9 %collective-permute-start.4 = (bf16[1,7,8,256]{3,2,1,0:T(8,128)(2,1)S(1)}, bf16[1,7,8,256]{3,2,1,0:T(8,128)(2,1)S(1)}, u32[]{:S(2)}, u32[]{:S(2)}) collective-permute-start(bf16[1,7,8,256]{3,2,1,0:T(8,128)(2,1)S(1)} %slice.527), channel_id=1, source_target_pairs={{2,0},{4,2},{6,4},{8,6},{10,8},{12,10},{14,12},{16,14},{18,16},{20... | collective-permute-start | bytes 86024 | tf_op jit(solution)/shard_map/ppermute | solution.py:20
  54.4 1.2 collective-permute-start.5
  57.0 55.7 %all-reduce.33.cloned.1.call-start = ((), (), s32[]{:S(2)}) async-start(), calls=%async_computation.2 | async-start | bytes 131072 | tf_op jit(solution)/shard_map/psum | solution.py:115
  77.9 1.3 collective-permute-start.6
  79.2 7.8 %collective-permute-start.7 = (f32[1,7,8,256]{3,2,1,0:T(8,128)S(1)}, f32[1,7,8,256]{3,2,1,0:T(8,128)S(1)}, u32[]{:S(2)}, u32[]{:S(2)}) collective-permute-start(f32[1,7,8,256]{3,2,1,0:T(8,128)S(1)} %slice.540), channel_id=1, source_target_pairs={{30,0},{0,2},{2,4},{4,6},{6,8},{8,10},{10,12},{12,14},{14,16},{16,... | collective-permute-start | bytes 172040 | tf_op jit(solution)/shard_map/ppermute | solution.py:20
  87.2 3.9 %collective-permute-start.8 = (bf16[1,7,8,256]{3,2,1,0:T(8,128)(2,1)S(1)}, bf16[1,7,8,256]{3,2,1,0:T(8,128)(2,1)S(1)}, u32[]{:S(2)}, u32[]{:S(2)}) collective-permute-start(bf16[1,7,8,256]{3,2,1,0:T(8,128)(2,1)S(1)} %slice.541), channel_id=1, source_target_pairs={{2,0},{4,2},{6,4},{8,6},{10,8},{12,10},{14,12},{16,14},{18,16},{20... | collective-permute-start | bytes 86024 | tf_op jit(solution)/shard_map/ppermute | solution.py:20
  91.1 1.2 collective-permute-start.9
  93.7 55.8 %all-reduce.35.cloned.1.call-start = ((), (), s32[]{:S(2)}) async-start(), calls=%async_computation.3 | async-start | bytes 131072 | tf_op jit(solution)/shard_map/psum | solution.py:115
  114.6 1.3 collective-permute-start.10
  115.9 7.8 %collective-permute-start.11 = (f32[1,7,8,256]{3,2,1,0:T(8,128)S(1)}, f32[1,7,8,256]{3,2,1,0:T(8,128)S(1)}, u32[]{:S(2)}, u32[]{:S(2)}) collective-permute-start(f32[1,7,8,256]{3,2,1,0:T(8,128)S(1)} %slice.554), channel_id=1, source_target_pairs={{30,0},{0,2},{2,4},{4,6},{6,8},{8,10},{10,12},{12,14},{14,16},{16,... | collective-permute-start | bytes 172040 | tf_op jit(solution)/shard_map/ppermute | solution.py:20
  124.0 3.9 %collective-permute-start.12 = (bf16[1,7,8,256]{3,2,1,0:T(8,128)(2,1)S(1)}, bf16[1,7,8,256]{3,2,1,0:T(8,128)(2,1)S(1)}, u32[]{:S(2)}, u32[]{:S(2)}) collective-permute-start(bf16[1,7,8,256]{3,2,1,0:T(8,128)(2,1)S(1)} %slice.555), channel_id=1, source_target_pairs={{2,0},{4,2},{6,4},{8,6},{10,8},{12,10},{14,12},{16,14},{18,16},{20... | collective-permute-start | bytes 86024 | tf_op jit(solution)/shard_map/ppermute | solution.py:20
  127.9 1.2 collective-permute-start.13
  151.4 1.3 collective-permute-start.14
  152.7 7.8 %collective-permute-start.15 = (f32[1,7,8,256]{3,2,1,0:T(8,128)S(1)}, f32[1,7,8,256]{3,2,1,0:T(8,128)S(1)}, u32[]{:S(2)}, u32[]{:S(2)}) collective-permute-start(f32[1,7,8,256]{3,2,1,0:T(8,128)S(1)} %slice.568), channel_id=1, source_target_pairs={{30,0},{0,2},{2,4},{4,6},{6,8},{8,10},{10,12},{12,14},{14,16},{16,... | collective-permute-start | bytes 172040 | tf_op jit(solution)/shard_map/ppermute | solution.py:20
Sparse Core Ops, SparseCore 0:
  19.9 19.4 all-reduce.28
  57.1 18.8 all-reduce.30
  93.8 18.8 all-reduce.32
  130.6 18.8 all-reduce.34
where the time goes:
time: 168 us
  waiting for transfers between devices  115 us (68%)
  starting transfers between devices  20.9 us (12%)
  between operations  13.9 us (8%)
  matrix products  11.4 us (7%)
  local copies, waits for them, and re-layouts  4.82 us (3%)
  other arithmetic  2.15 us (1%)
    psum x4, waiting for transfers between devices, reduce_sum(): return lax.psum(local_sum, 'gy')  75.1 us
    ppermute x16, waiting for transfers between devices, from_behind(): return lax.ppermute(block, axis, route)  39.7 us
    ppermute x16, starting transfers between devices, from_behind(): return lax.ppermute(block, axis, route)  20.8 us
    dot_general x4, matrix products, cell_terms(): jnp.einsum('ksp,po->kso', onehot, weights, precision=lax.Precision.HIGHEST)  4.22 us
    dot_general x4, matrix products, cell_terms(): jnp.einsum('ksp,kso->po', onehot, coefficient, precision=lax.Precision.HI...  3.77 us
  transfers between devices with their start and end apart: 20, of which 20 were waited for; matrix products, arithmetic and copies ran while one was open for 2% of the time, Pallas kernels for 0%

commit v1 on v0

v1 whole, which is shorter than its diff:
```python
import functools

import jax
import jax.numpy as jnp
from jax import lax
from jax.experimental import pallas as pl
from jax.experimental.pallas import tpu as pltpu
from jax.sharding import PartitionSpec as P

STEPS = 4
BLOCKS = 2
CENTER = 5.0
HALF_WIDTH = 9.0
MESH = pl.DeviceIdType.MESH
F32 = jnp.float32
BF16 = jnp.bfloat16

ROUTES = ((1, 0), (-1, 0), (0, 1), (0, -1), (1, 1), (1, -1), (-1, 1), (-1, -1))
FORWARD = (0, 2, 4)


def mm(a, b):
    return jnp.dot(a, b, preferred_element_type=F32)


def kernel(
    nx, ny,
    x_hbm, ham_hbm, proj_hbm, ids_hbm, cpl_hbm, out_hbm,
    x_v, ham_v, proj_v, ids_v, cpl_v, out_v,
    state, w, u, rows_v, cols_v,
    halo_s, halo_r, halo_cs, halo_cr,
    face_s, face_r, corner_s, corner_r, sum_s, sum_r,
    in_sem, out_sem, halo_ss, halo_rs, face_ss, face_rs, sum_ss, sum_rs,
):
    points = w.shape[1]
    last = points - 1
    width = w.shape[-1]
    face = points * points
    gx, gy = lax.axis_index("gx"), lax.axis_index("gy")

    def device(dx, dy):
        return (lax.rem(gx + nx + dx, nx), lax.rem(gy + ny + dy, ny))

    def split(value):
        return value.reshape(points, points, width)

    loads = [
        pltpu.make_async_copy(src, dst, in_sem.at[k])
        for k, (src, dst) in enumerate(
            ((x_hbm, x_v), (proj_hbm, proj_v), (ids_hbm, ids_v), (cpl_hbm, cpl_v), (ham_hbm, ham_v))
        )
    ]
    for load in loads:
        load.start()

    barrier = pltpu.get_barrier_semaphore()
    greeted = list(ROUTES) + [(0, k) for k in range(2, ny - 1)]
    for dx, dy in greeted:
        pl.semaphore_signal(barrier, inc=1, device_id=device(dx, dy), device_id_type=MESH)

    loads[0].wait()
    x = x_v[...].astype(F32)
    pad = jnp.zeros((points, x.shape[-1]), F32)
    halo_s[0] = jnp.concatenate([x[0].reshape(last * points, -1), pad], 0).astype(BF16)
    halo_s[1] = jnp.concatenate([x[:, 0].reshape(last * points, -1), pad], 0).astype(BF16)
    halo_cs[...] = x[0, 0]

    pl.semaphore_wait(barrier, len(greeted))

    halos = []
    for k, (src, dst, route) in enumerate(
        (
            (halo_s.at[0], halo_r.at[0], (-1, 0)),
            (halo_s.at[1], halo_r.at[1], (0, -1)),
            (halo_cs, halo_cr, (-1, -1)),
        )
    ):
        halos.append(
            pltpu.make_async_remote_copy(
                src, dst, halo_ss.at[k], halo_rs.at[k], device_id=device(*route), device_id_type=MESH
            )
        )
        halos[-1].start()

    for blk in range(BLOCKS):
        state[0, blk, :last, :last] = x[..., blk * width : (blk + 1) * width]

    for load in loads[1:]:
        load.wait()
    group = cpl_v.shape[-1]
    slots = ids_v.shape[-1]
    onehot = (lax.broadcasted_iota(jnp.int32, (group, slots), 0) == ids_v[0]).astype(F32).astype(BF16)
    rows = mm(onehot, proj_v[0, 0])
    high = rows.astype(BF16).astype(F32)
    both = jnp.concatenate([high, rows - high], 0)
    rows_v[...] = both.astype(BF16)
    cols_v[...] = both.T.astype(BF16)
    square = (group, group)
    eye = lax.broadcasted_iota(jnp.int32, square, 0) == lax.broadcasted_iota(jnp.int32, square, 1)
    strength = jnp.sum(jnp.where(eye, cpl_v[...], 0.0), axis=1, keepdims=True)

    for copy in halos:
        copy.wait_recv()
    for blk in range(BLOCKS):
        cut = slice(blk * width, (blk + 1) * width)
        ahead = halo_r[0, :, cut].astype(F32)
        beside = halo_r[1, :, cut].astype(F32)
        state[0, blk, last, :last] = split(ahead)[:last]
        state[0, blk, :last, last] = split(beside)[:last]
        state[0, blk, last, last] = halo_cr[:, cut]

    sent = list(halos)
    faces = {}
    sums = {}

    def project(step, blk):
        u[blk] = state[step % 2, blk].reshape(points * face, width).astype(BF16)
        parts = mm(rows_v[...], u[blk])
        sum_s[step, blk] = parts[:group] + parts[group:]
        for k in range(1, ny):
            copy = pltpu.make_async_remote_copy(
                sum_s.at[step, blk],
                sum_r.at[step, blk, k - 1],
                sum_ss.at[step, blk, k - 1],
                sum_rs.at[step, blk, k - 1],
                device_id=device(0, k),
                device_id_type=MESH,
            )
            copy.start()
            sums[step, blk, k] = copy
            sent.append(copy)
        w[blk] = mm(ham_v[0, 0], u[blk]).reshape(points, points, points, width)

    def spread(step, blk):
        total = sum_s[step, blk]
        for k in range(1, ny):
            sums[step, blk, k].wait_recv()
            total = total + sum_r[step, blk, k - 1]
        weight = strength * total
        weight = jnp.concatenate([weight, weight], 0).astype(BF16)
        w[blk] = w[blk] + mm(cols_v[...], weight).reshape(points, points, points, width)
        final = step == STEPS - 1
        for d, (dx, dy) in enumerate(ROUTES):
            if final and d not in FORWARD:
                continue
            a = last if dx > 0 else 0
            b = last if dy > 0 else 0
            if d < 4:
                layer = w[blk, a] if dx else w[blk, :, b]
                face_s[step, blk, d] = layer.reshape(face, width).astype(BF16)
                src, dst = face_s.at[step, blk, d], face_r.at[step, blk, d]
            else:
                corner_s[step, blk, d - 4] = w[blk, a, b]
                src, dst = corner_s.at[step, blk, d - 4], corner_r.at[step, blk, d - 4]
            copy = pltpu.make_async_remote_copy(
                src,
                dst,
                face_ss.at[step, blk, d],
                face_rs.at[step, blk, d],
                device_id=device(dx, dy),
                device_id_type=MESH,
            )
            copy.start()
            faces[step, blk, d] = copy
            sent.append(copy)

    def combine(step, blk):
        final = step == STEPS - 1
        for d, (dx, dy) in enumerate(ROUTES):
            if final and d not in FORWARD:
                continue
            faces[step, blk, d].wait_recv()
            a = 0 if dx > 0 else last
            b = 0 if dy > 0 else last
            if d < 4:
                layer = split(face_r[step, blk, d].astype(F32))
                if dx:
                    w[blk, a] = w[blk, a] + layer
                else:
                    w[blk, :, b] = w[blk, :, b] + layer
            else:
                w[blk, a, b] = w[blk, a, b] + corner_r[step, blk, d - 4]
        now, other = step % 2, (step + 1) % 2
        if step == 0:
            state[other, blk] = (w[blk] - CENTER * state[now, blk]) * (1.0 / HALF_WIDTH)
        elif not final:
            state[other, blk] = (w[blk] - CENTER * state[now, blk]) * (2.0 / HALF_WIDTH) - state[other, blk]
        else:
            own = (slice(0, last), slice(0, last))
            out_v[:, :, :, blk * width : (blk + 1) * width] = (
                w[(blk,) + own] - CENTER * state[(now, blk) + own]
            ) * (2.0 / HALF_WIDTH) - state[(other, blk) + own]

    for step in range(STEPS):
        for blk in range(BLOCKS):
            if step:
                combine(step - 1, blk)
            project(step, blk)
        for blk in range(BLOCKS):
            spread(step, blk)
    for blk in range(BLOCKS):
        combine(STEPS - 1, blk)

    store = pltpu.make_async_copy(out_v, out_hbm, out_sem)
    store.start()
    for copy in sent:
        copy.wait_send()
    store.wait()


def per_device(nx, ny, orbitals, cell_ham, proj_vals, proj_ids, coupling):
    last, _, points, orbs = orbitals.shape
    nodes = cell_ham.shape[-1]
    slots = proj_vals.shape[-2]
    group = coupling.shape[-1]
    width = orbs // BLOCKS
    face = points * points
    field = (BLOCKS, points, points, points, width)
    dma = pltpu.SemaphoreType.DMA
    scratch = [
        pltpu.VMEM(orbitals.shape, BF16),
        pltpu.VMEM(cell_ham.shape, BF16),
        pltpu.VMEM(proj_vals.shape, BF16),
        pltpu.VMEM(proj_ids.shape, jnp.int32),
        pltpu.VMEM(coupling.shape, F32),
        pltpu.VMEM(orbitals.shape, F32),
        pltpu.VMEM((2,) + field, F32),
        pltpu.VMEM(field, F32),
        pltpu.VMEM((BLOCKS, nodes, width), BF16),
        pltpu.VMEM((2 * group, nodes), BF16),
        pltpu.VMEM((nodes, 2 * group), BF16),
        pltpu.VMEM((2, face, orbs), BF16),
        pltpu.VMEM((2, face, orbs), BF16),
        pltpu.VMEM((points, orbs), F32),
        pltpu.VMEM((points, orbs), F32),
        pltpu.VMEM((STEPS, BLOCKS, 4, face, width), BF16),
        pltpu.VMEM((STEPS, BLOCKS, 4, face, width), BF16),
        pltpu.VMEM((STEPS, BLOCKS, 4, points, width), F32),
        pltpu.VMEM((STEPS, BLOCKS, 4, points, width), F32),
        pltpu.VMEM((STEPS, BLOCKS, group, width), F32),
        pltpu.VMEM((STEPS, BLOCKS, ny - 1, group, width), F32),
        dma((5,)),
        dma,
        dma((3,)),
        dma((3,)),
        dma((STEPS, BLOCKS, 8)),
        dma((STEPS, BLOCKS, 8)),
        dma((STEPS, BLOCKS, ny - 1)),
        dma((STEPS, BLOCKS, ny - 1)),
    ]
    anywhere = pl.BlockSpec(memory_space=pl.ANY)
    return pl.pallas_call(
        functools.partial(kernel, nx, ny),
        out_shape=jax.ShapeDtypeStruct(orbitals.shape, F32),
        in_specs=[anywhere] * 5,
        out_specs=anywhere,
        scratch_shapes=scratch,
        compiler_params=pltpu.CompilerParams(
            collective_id=0, has_side_effects=True, vmem_limit_bytes=32 * 2**20
        ),
        cost_estimate=pl.CostEstimate(
            flops=2 * STEPS * nodes * (nodes + 4 * group) * orbs,
            bytes_accessed=2 * nodes * nodes + 6 * nodes * orbs,
            transcendentals=0,
        ),
    )(orbitals, cell_ham, proj_vals, proj_ids, coupling)


def solution(mesh):
    placed = (
        P("gx", "gy", None, None),
        P("gx", "gy", None, None),
        P("gx", "gy", None, None),
        P("gx", "gy", None),
        P("gx", None),
    )
    return jax.shard_map(
        functools.partial(per_device, mesh.shape["gx"], mesh.shape["gy"]),
        mesh=mesh, in_specs=placed, out_specs=P("gx", "gy", None, None), check_vma=False,
    )
```

time: 168 us -> 40.2 us (0.24)
  waiting for transfers between devices: 115 us -> 0 us
  Pallas kernels: 0 us -> 35.1 us
  starting transfers between devices: 20.9 us -> 0 us
  between operations: 13.9 us -> 0.01 us
  matrix products: 11.4 us -> 0 us
  other arithmetic: 2.15 us -> 0 us
    psum x4 -> x0, waiting for transfers between devices: 75.1 us -> none  [reduce_sum(): return lax.psum(local_sum, 'gy')]
    ppermute x16 -> x0, waiting for transfers between devices: 39.7 us -> none  [from_behind(): return lax.ppermute(block, axis, route)]
    pallas_call x0 -> x1, Pallas kernels: none -> 35.1 us  [per_device(): pl.pallas_call(functools.partial(kernel, nx, ny), out_shape=jax.ShapeDtyp...]
    ppermute x16 -> x0, starting transfers between devices: 20.8 us -> none  [from_behind(): return lax.ppermute(block, axis, route)]
    dot_general x20 -> x0, matrix products: 11.4 us -> none  [the longest x4 4.22 us: cell_terms(): jnp.einsum('ksp,po->kso', onehot, weights, precision=lax.Precision.HIGHEST)]
    unnamed x11, local copies, waits for them, and re-layouts: 2.33 us -> 4.79 us
  transfers between devices with their start and end apart: 20 -> 0, of which waited for: 20 -> 0; matrix products, arithmetic and copies ran while one was open for 2% -> 0% of each run, Pallas kernels for 0% -> 0%
where the time goes in v1:
time: 40.2 us; the launch traced here: 39.9 us
  Pallas kernels  35.1 us (87%)
  local copies, waits for them, and re-layouts  4.79 us (12%)
    pallas_call x1, Pallas kernels, per_device(): pl.pallas_call(functools.partial(kernel, nx, ny), out_shape=jax.ShapeDtyp...  35.1 us
    unnamed x11, local copies, waits for them, and re-layouts  4.79 us

profile of v1, /device:TPU:0, one launch (start us, length us, event | category | flops | bytes accessed | tf_op | source)
XLA Modules:
  0.0 39.9 jit_solution(3935715750547196108)
XLA Ops:
  0.0 0.0 copy-start
  0.0 1.0 %copy-done = bf16[1,1,512,512]{3,2,1,0:T(8,128)(2,1)S(1)} copy-done((bf16[1,1,512,512]{3,2,1,0:T(8,128)(2,1)S(1)}, bf16[1,1,512,512]{3,2,1,0:T(8,128)(2,1)}, u32[]{:S(2)}) %copy-start) | copy-done | bytes 524312
  1.0 0.0 copy-start.1
  1.0 0.9 %copy-done.1 = bf16[7,7,8,256]{3,2,1,0:T(8,128)(2,1)S(1)} copy-done((bf16[7,7,8,256]{3,2,1,0:T(8,128)(2,1)S(1)}, bf16[7,7,8,256]{3,2,1,0:T(8,128)(2,1)}, u32[]{:S(2)}) %copy-start.1) | copy-done | bytes 200728
  2.0 0.0 copy-start.2
  2.0 0.8 %copy-done.2 = bf16[1,1,32,512]{3,2,1,0:T(8,128)(2,1)S(1)} copy-done((bf16[1,1,32,512]{3,2,1,0:T(8,128)(2,1)S(1)}, bf16[1,1,32,512]{3,2,1,0:T(8,128)(2,1)}, u32[]{:S(2)}) %copy-start.2) | copy-done | bytes 32792
  2.7 0.0 copy-start.3
  2.7 0.7 %copy-done.3 = s32[1,1,32]{2,1,0:T(1,128)S(1)} copy-done((s32[1,1,32]{2,1,0:T(1,128)S(1)}, s32[1,1,32]{2,1,0:T(1,128)}, u32[]{:S(2)}) %copy-start.3) | copy-done | bytes 152
  3.4 0.0 copy-start.4
  3.4 0.7 %copy-done.4 = f32[1,64]{1,0:T(1,128)S(1)} copy-done((f32[1,64]{1,0:T(1,128)S(1)}, f32[1,64]{1,0:T(1,128)}, u32[]{:S(2)}) %copy-start.4) | copy-done | bytes 280
  4.0 35.1 %shard_map.55 = f32[7,7,8,256]{3,2,1,0:T(8,128)S(1)} custom-call(bf16[7,7,8,256]{3,2,1,0:T(8,128)(2,1)S(1)} %copy-done.1, bf16[1,1,512,512]{3,2,1,0:T(8,128)(2,1)S(1)} %copy-done, bf16[1,1,32,512]{3,2,1,0:T(8,128)(2,1)S(1)} %copy-done.2, s32[1,1,32]{2,1,0:T(1,128)S(1)} %copy-done.3, f32[1,64]{1,0:T(1,128)S(1)} %copy-done.4), custom_call_target="tpu_custom_call" | custom-call | flops 805306368 | bytes 1310720 | tf_op jit(solution)/shard_map/pallas_call | solution.py:252
  39.1 0.8 %copy.7 = f32[7,7,8,256]{3,2,1,0:T(8,128)} copy(f32[7,7,8,256]{3,2,1,0:T(8,128)S(1)} %shard_map.55) | data formatting | bytes 802816
Async XLA Ops:
  0.0 1.0 %copy-start = (bf16[1,1,512,512]{3,2,1,0:T(8,128)(2,1)S(1)}, bf16[1,1,512,512]{3,2,1,0:T(8,128)(2,1)}, u32[]{:S(2)}) copy-start(bf16[1,1,512,512]{3,2,1,0:T(8,128)(2,1)} %ham_hbm.1) | copy-start | bytes 1572868
  1.0 0.9 %copy-start.1 = (bf16[7,7,8,256]{3,2,1,0:T(8,128)(2,1)S(1)}, bf16[7,7,8,256]{3,2,1,0:T(8,128)(2,1)}, u32[]{:S(2)}) copy-start(bf16[7,7,8,256]{3,2,1,0:T(8,128)(2,1)} %x_hbm.1) | copy-start | bytes 602116
  2.0 0.8 %copy-start.2 = (bf16[1,1,32,512]{3,2,1,0:T(8,128)(2,1)S(1)}, bf16[1,1,32,512]{3,2,1,0:T(8,128)(2,1)}, u32[]{:S(2)}) copy-start(bf16[1,1,32,512]{3,2,1,0:T(8,128)(2,1)} %proj_hbm.1) | copy-start | bytes 98308
  2.7 0.7 %copy-start.3 = (s32[1,1,32]{2,1,0:T(1,128)S(1)}, s32[1,1,32]{2,1,0:T(1,128)}, u32[]{:S(2)}) copy-start(s32[1,1,32]{2,1,0:T(1,128)} %ids_hbm.1) | copy-start | bytes 388
  3.4 0.7 %copy-start.4 = (f32[1,64]{1,0:T(1,128)S(1)}, f32[1,64]{1,0:T(1,128)}, u32[]{:S(2)}) copy-start(f32[1,64]{1,0:T(1,128)} %cpl_hbm.1) | copy-start | bytes 772

commit v2 on v1

v2 whole, which is shorter than its diff:
```python
import functools

import jax
import jax.numpy as jnp
from jax import lax
from jax.experimental import pallas as pl
from jax.experimental.pallas import tpu as pltpu
from jax.sharding import PartitionSpec as P

STEPS = 4
CENTER = 5.0
HALF_WIDTH = 9.0
MESH = pl.DeviceIdType.MESH
F32 = jnp.float32
BF16 = jnp.bfloat16

ROUTES = ((1, 0), (-1, 0), (0, 1), (0, -1))
FORWARD = (0, 2)


def mm(a, b):
    return jnp.dot(a, b, preferred_element_type=F32)


def kernel(
    nx, ny,
    x_hbm, ham_hbm, proj_hbm, ids_hbm, cpl_hbm, out_hbm,
    x_v, ham_v, proj_v, ids_v, cpl_v, out_v,
    state, w, u, rows_v, cols_v, g_v, gy_s, gy_r,
    halo_s, halo_r, halo_cs, halo_cr,
    face_s, face_r, line_s, line_r, sum_s, sum_r,
    in_sem, out_sem, send_sem, recv_sem,
):
    points = w.shape[0]
    last = points - 1
    width = w.shape[-1]
    face = points * points
    gx, gy = lax.axis_index("gx"), lax.axis_index("gy")
    sent = []

    def device(dx, dy):
        return (lax.rem(gx + nx + dx, nx), lax.rem(gy + ny + dy, ny))

    def send(src, dst, route):
        k = len(sent)
        copy = pltpu.make_async_remote_copy(
            src, dst, send_sem.at[k], recv_sem.at[k], device_id=device(*route), device_id_type=MESH
        )
        copy.start()
        sent.append(copy)
        return copy

    def split(value):
        return value.reshape(points, points, value.shape[-1])

    def in_two(value):
        high = value.astype(BF16).astype(F32)
        lane = lax.broadcasted_iota(jnp.int32, value.shape, 1)
        return jnp.where(lane < value.shape[1] // 2, high, value - high).astype(BF16)

    loads = [
        pltpu.make_async_copy(src, dst, in_sem.at[k])
        for k, (src, dst) in enumerate(
            ((x_hbm, x_v), (proj_hbm, proj_v), (ids_hbm, ids_v), (cpl_hbm, cpl_v), (ham_hbm, ham_v))
        )
    ]
    for load in loads:
        load.start()

    barrier = pltpu.get_barrier_semaphore()
    greeted = list(ROUTES) + [(1, 1), (-1, -1)] + [(0, k) for k in range(2, ny - 1)]
    for dx, dy in greeted:
        pl.semaphore_signal(barrier, inc=1, device_id=device(dx, dy), device_id_type=MESH)

    loads[0].wait()
    x = x_v[...].astype(F32)
    pad = jnp.zeros((points, width), F32)
    halo_s[0] = jnp.concatenate([x[0].reshape(last * points, width), pad], 0).astype(BF16)
    halo_s[1] = jnp.concatenate([x[:, 0].reshape(last * points, width), pad], 0).astype(BF16)
    halo_cs[...] = x[0, 0]

    pl.semaphore_wait(barrier, len(greeted))
    halos = [
        send(halo_s.at[0], halo_r.at[0], (-1, 0)),
        send(halo_cs, halo_cr, (-1, -1)),
        send(halo_s.at[1], halo_r.at[1], (0, -1)),
    ]
    state[0, :last, :last] = x

    for load in loads[1:]:
        load.wait()
    group = cpl_v.shape[-1]
    slots = ids_v.shape[-1]
    onehot = (lax.broadcasted_iota(jnp.int32, (group, slots), 0) == ids_v[0]).astype(F32).astype(BF16)
    rows = mm(onehot, proj_v[0, 0])
    high = rows.astype(BF16).astype(F32)
    rows_v[...] = jnp.concatenate([high, rows - high], 0).astype(BF16)
    square = (group, group)
    eye = lax.broadcasted_iota(jnp.int32, square, 0) == lax.broadcasted_iota(jnp.int32, square, 1)
    strength = jnp.sum(jnp.where(eye, cpl_v[...], 0.0), axis=1, keepdims=True)
    scaled = strength * rows
    g_v[...] = jnp.concatenate([scaled, scaled], 0).T.reshape(g_v.shape)

    gy_s[0] = g_v[:, last].reshape(face, 2 * group)
    gy_s[1] = g_v[:, 0].reshape(face, 2 * group)
    sides = [send(gy_s.at[0], gy_r.at[0], (0, 1)), send(gy_s.at[1], gy_r.at[1], (0, -1))]
    for k, b in enumerate((0, last)):
        sides[k].wait_recv()
        g_v[:, b] = g_v[:, b] + split(gy_r[k])
    cols_v[...] = in_two(g_v[...].reshape(points * face, 2 * group))

    halos[2].wait_recv()
    state[0, :last, last] = split(halo_r[1].astype(F32))[:last]
    halos[0].wait_recv()
    halos[1].wait_recv()
    state[0, last, :last] = split(halo_r[0].astype(F32))[:last]
    state[0, last, last] = halo_cr[...]
    u[...] = state[0].reshape(points * face, width).astype(BF16)

    def twice(total):
        total = total.astype(BF16).astype(F32)
        return jnp.concatenate([total, total], 0).astype(BF16)

    for step in range(STEPS):
        final = step == STEPS - 1
        now, other = step % 2, (step + 1) % 2
        scale = (1.0 if step == 0 else 2.0) / HALF_WIDTH
        faces, sums = {}, {}

        def send_face(d, layer):
            face_s[step, d] = layer.reshape(face, width).astype(BF16)
            faces[d] = send(face_s.at[step, d], face_r.at[step, d], ROUTES[d])

        parts = mm(rows_v[...], u[...])
        local = parts[:group] + parts[group:]
        sum_s[step] = local.astype(BF16)
        for k in range(1, ny):
            sums[k] = send(sum_s.at[step], sum_r.at[step, k - 1], (0, k))
        w[last] = split(mm(ham_v[0, 0, last * face :], u[...]))
        w[0] = split(mm(ham_v[0, 0, :face], u[...]))
        lines = []
        for k, dy in enumerate((1,) if final else (1, -1)):
            b = last if dy > 0 else 0
            line_s[step, k, 0] = w[0, b]
            line_s[step, k, 1] = w[last, b]
            lines.append(send(line_s.at[step, k], line_r.at[step, k], (0, dy)))
        inner = slice(face, last * face)
        w[1:last] = mm(ham_v[0, 0, inner], u[...]).reshape(last - 1, points, points, width)
        send_face(2, w[:, last])
        if not final:
            send_face(3, w[:, 0])
        total = local
        for k in range(1, ny):
            sums[k].wait_recv()
            total = total + sum_r[step, k - 1].astype(F32)
        total = twice(total)
        w[last] = w[last] + split(mm(cols_v[last * face :], total))
        w[0] = w[0] + split(mm(cols_v[:face], total))
        for k, line in enumerate(lines):
            line.wait_recv()
            b = 0 if k == 0 else last
            w[0, b] = w[0, b] + line_r[step, k, 0]
            w[last, b] = w[last, b] + line_r[step, k, 1]
        send_face(0, w[last])
        if not final:
            send_face(1, w[0])

        w[1:last] = w[1:last] + mm(cols_v[inner], total).reshape(last - 1, points, points, width)
        held = last if final else points
        fresh = (w[:held] - CENTER * state[now, :held]) * scale
        if step:
            fresh = fresh - state[other, :held]
        state[other, :held] = fresh
        for d in (2,) if final else (2, 3):
            faces[d].wait_recv()
            b = 0 if d == 2 else last
            layer = split(face_r[step, d].astype(F32))[1:last]
            state[other, 1:last, b] = state[other, 1:last, b] + scale * layer
        if final:
            out_v[1:] = state[other, 1:last, :last]
            store_rest = pltpu.make_async_copy(out_v.at[pl.ds(1, last - 1)], out_hbm.at[pl.ds(1, last - 1)], out_sem.at[0])
            store_rest.start()
        else:
            u[face : last * face] = state[other, 1:last].reshape((last - 1) * face, width).astype(BF16)

        for k, dx in enumerate((1,) if final else (1, -1)):
            a = 0 if dx > 0 else last
            faces[k].wait_recv()
            layer = split(face_r[step, k].astype(F32))
            state[other, a] = state[other, a] + scale * layer
            if not final:
                u[a * face : (a + 1) * face] = state[other, a].reshape(face, width).astype(BF16)
        if final:
            out_v[0] = state[other, 0, :last]

    store = pltpu.make_async_copy(out_v.at[pl.ds(0, 1)], out_hbm.at[pl.ds(0, 1)], out_sem.at[1])
    store.start()
    for copy in sent:
        copy.wait_send()
    store_rest.wait()
    store.wait()


def per_device(nx, ny, orbitals, cell_ham, proj_vals, proj_ids, coupling):
    last, _, points, width = orbitals.shape
    nodes = cell_ham.shape[-1]
    group = coupling.shape[-1]
    face = points * points
    field = (points, points, points, width)
    messages = 5 + STEPS * (len(ROUTES) + 2 + ny - 1)
    dma = pltpu.SemaphoreType.DMA
    scratch = [
        pltpu.VMEM(orbitals.shape, BF16),
        pltpu.VMEM(cell_ham.shape, BF16),
        pltpu.VMEM(proj_vals.shape, BF16),
        pltpu.VMEM(proj_ids.shape, jnp.int32),
        pltpu.VMEM(coupling.shape, F32),
        pltpu.VMEM(orbitals.shape, F32),
        pltpu.VMEM((2,) + field, F32),
        pltpu.VMEM(field, F32),
        pltpu.VMEM((nodes, width), BF16),
        pltpu.VMEM((2 * group, nodes), BF16),
        pltpu.VMEM((nodes, 2 * group), BF16),
        pltpu.VMEM((points, points, points, 2 * group), F32),
        pltpu.VMEM((2, face, 2 * group), F32),
        pltpu.VMEM((2, face, 2 * group), F32),
        pltpu.VMEM((2, face, width), BF16),
        pltpu.VMEM((2, face, width), BF16),
        pltpu.VMEM((points, width), F32),
        pltpu.VMEM((points, width), F32),
        pltpu.VMEM((STEPS, 4, face, width), BF16),
        pltpu.VMEM((STEPS, 4, face, width), BF16),
        pltpu.VMEM((STEPS, 2, 2, points, width), F32),
        pltpu.VMEM((STEPS, 2, 2, points, width), F32),
        pltpu.VMEM((STEPS, group, width), BF16),
        pltpu.VMEM((STEPS, ny - 1, group, width), BF16),
        dma((5,)),
        dma((2,)),
        dma((messages,)),
        dma((messages,)),
    ]
    anywhere = pl.BlockSpec(memory_space=pl.ANY)
    return pl.pallas_call(
        functools.partial(kernel, nx, ny),
        out_shape=jax.ShapeDtypeStruct(orbitals.shape, F32),
        in_specs=[pl.BlockSpec(memory_space=pltpu.HBM)] * 5,
        out_specs=anywhere,
        scratch_shapes=scratch,
        compiler_params=pltpu.CompilerParams(
            collective_id=0, has_side_effects=True, vmem_limit_bytes=60 * 2**20
        ),
        cost_estimate=pl.CostEstimate(
            flops=2 * STEPS * nodes * (nodes + 4 * group) * width,
            bytes_accessed=2 * nodes * nodes + 6 * nodes * width,
            transcendentals=0,
        ),
    )(orbitals, cell_ham, proj_vals, proj_ids, coupling)


def solution(mesh):
    placed = (
        P("gx", "gy", None, None),
        P("gx", "gy", None, None),
        P("gx", "gy", None, None),
        P("gx", "gy", None),
        P("gx", None),
    )
    return jax.shard_map(
        functools.partial(per_device, mesh.shape["gx"], mesh.shape["gy"]),
        mesh=mesh, in_specs=placed, out_specs=P("gx", "gy", None, None), check_vma=False,
    )
```

time: 40.2 us -> 35.5 us (0.88)
  local copies, waits for them, and re-layouts: 4.79 us -> 1.77 us
  Pallas kernels: 35.1 us -> 33.5 us
    unnamed x11 -> x1, local copies, waits for them, and re-layouts: 4.79 us -> 1.77 us
    pallas_call x1, Pallas kernels: 35.1 us -> 33.5 us  [per_device(): pl.pallas_call(functools.partial(kernel, nx, ny), out_shape=jax.ShapeDtyp...]
where the time goes in v2:
time: 35.5 us; the launch traced here: 35.3 us
  Pallas kernels  33.5 us (94%)
  local copies, waits for them, and re-layouts  1.77 us (5%)
    pallas_call x1, Pallas kernels, per_device(): pl.pallas_call(functools.partial(kernel, nx, ny), out_shape=jax.ShapeDtyp...  33.5 us
    unnamed x1, local copies, waits for them, and re-layouts  1.77 us

profile of v2, /device:TPU:0, one launch (start us, length us, event | category | flops | bytes accessed | tf_op | source)
XLA Modules:
  0.0 35.3 jit_solution(16807766791109707650)
XLA Ops:
  0.0 33.5 %shard_map.55 = f32[7,7,8,256]{3,2,1,0:T(8,128)} custom-call(bf16[7,7,8,256]{3,2,1,0:T(8,128)(2,1)} %x_hbm.1, bf16[1,1,512,512]{3,2,1,0:T(8,128)(2,1)} %ham_hbm.1, bf16[1,1,32,512]{3,2,1,0:T(8,128)(2,1)} %proj_hbm.1, s32[1,1,32]{2,1,0:T(1,128)} %ids_hbm.1, f32[1,64]{1,0:T(1,128)} %cpl_hbm.1), custom_call_target="tpu_custom_call" | custom-call | flops 805306368 | bytes 1310720 | tf_op jit(solution)/shard_map/pallas_call | solution.py:243
  33.5 1.8 %copy.7 = f32[7,7,8,256]{3,2,1,0:T(8,128)} copy(f32[7,7,8,256]{3,2,1,0:T(8,128)} %shard_map.55) | data formatting | bytes 802816

commit v3 on v2

--- a/solution.py
+++ b/solution.py
@@ -24,12 +24,12 @@
 
 def kernel(
     nx, ny,
-    x_hbm, ham_hbm, proj_hbm, ids_hbm, cpl_hbm, out_hbm,
-    x_v, ham_v, proj_v, ids_v, cpl_v, out_v,
+    x_hbm, ham_hbm, proj_hbm, ids_hbm, cpl_hbm, out_v,
+    x_v, ham_v, proj_v, ids_v, cpl_v,
     state, w, u, rows_v, cols_v, g_v, gy_s, gy_r,
     halo_s, halo_r, halo_cs, halo_cr,
     face_s, face_r, line_s, line_r, sum_s, sum_r,
-    in_sem, out_sem, send_sem, recv_sem,
+    in_sem, send_sem, recv_sem,
 ):
     points = w.shape[0]
     last = points - 1
@@ -178,8 +178,6 @@
             state[other, 1:last, b] = state[other, 1:last, b] + scale * layer
         if final:
             out_v[1:] = state[other, 1:last, :last]
-            store_rest = pltpu.make_async_copy(out_v.at[pl.ds(1, last - 1)], out_hbm.at[pl.ds(1, last - 1)], out_sem.at[0])
-            store_rest.start()
         else:
             u[face : last * face] = state[other, 1:last].reshape((last - 1) * face, width).astype(BF16)
 
@@ -193,12 +191,8 @@
         if final:
             out_v[0] = state[other, 0, :last]
 
-    store = pltpu.make_async_copy(out_v.at[pl.ds(0, 1)], out_hbm.at[pl.ds(0, 1)], out_sem.at[1])
-    store.start()
     for copy in sent:
         copy.wait_send()
-    store_rest.wait()
-    store.wait()
 
 
 def per_device(nx, ny, orbitals, cell_ham, proj_vals, proj_ids, coupling):
@@ -215,7 +209,6 @@
         pltpu.VMEM(proj_vals.shape, BF16),
         pltpu.VMEM(proj_ids.shape, jnp.int32),
         pltpu.VMEM(coupling.shape, F32),
-        pltpu.VMEM(orbitals.shape, F32),
         pltpu.VMEM((2,) + field, F32),
         pltpu.VMEM(field, F32),
         pltpu.VMEM((nodes, width), BF16),
@@ -235,19 +228,18 @@
         pltpu.VMEM((STEPS, group, width), BF16),
         pltpu.VMEM((STEPS, ny - 1, group, width), BF16),
         dma((5,)),
-        dma((2,)),
         dma((messages,)),
         dma((messages,)),
     ]
     anywhere = pl.BlockSpec(memory_space=pl.ANY)
     return pl.pallas_call(
         functools.partial(kernel, nx, ny),
-        out_shape=jax.ShapeDtypeStruct(orbitals.shape, F32),
+        out_shape=pltpu.VMEM(orbitals.shape, F32),
         in_specs=[pl.BlockSpec(memory_space=pltpu.HBM)] * 5,
-        out_specs=anywhere,
+        out_specs=pl.BlockSpec(memory_space=pltpu.VMEM),
         scratch_shapes=scratch,
         compiler_params=pltpu.CompilerParams(
-            collective_id=0, has_side_effects=True, vmem_limit_bytes=60 * 2**20
+            collective_id=0, has_side_effects=True, vmem_limit_bytes=56 * 2**20
         ),
         cost_estimate=pl.CostEstimate(
             flops=2 * STEPS * nodes * (nodes + 4 * group) * width,

time: 35.5 us -> 33.9 us (0.955)
  local copies, waits for them, and re-layouts: 1.77 us -> 0.75 us
  Pallas kernels: 33.5 us -> 33 us
    unnamed x1, local copies, waits for them, and re-layouts: 1.77 us -> 0.75 us
    pallas_call x1, Pallas kernels: 33.5 us -> 33 us  [per_device(): pl.pallas_call(functools.partial(kernel, nx, ny), out_shape=pltpu.VMEM(or...]
where the time goes in v3:
time: 33.9 us; the launch traced here: 33.8 us
  Pallas kernels  33 us (97%)
  local copies, waits for them, and re-layouts  0.75 us (2%)
    pallas_call x1, Pallas kernels, per_device(): pl.pallas_call(functools.partial(kernel, nx, ny), out_shape=pltpu.VMEM(or...  33 us
    unnamed x1, local copies, waits for them, and re-layouts  0.75 us

profile of v3, /device:TPU:0, one launch (start us, length us, event | category | flops | bytes accessed | tf_op | source)
XLA Modules:
  0.0 33.8 jit_solution(365648308115625800)
XLA Ops:
  0.0 33.0 %shard_map.55 = f32[7,7,8,256]{3,2,1,0:T(8,128)S(1)} custom-call(bf16[7,7,8,256]{3,2,1,0:T(8,128)(2,1)} %x_hbm.1, bf16[1,1,512,512]{3,2,1,0:T(8,128)(2,1)} %ham_hbm.1, bf16[1,1,32,512]{3,2,1,0:T(8,128)(2,1)} %proj_hbm.1, s32[1,1,32]{2,1,0:T(1,128)} %ids_hbm.1, f32[1,64]{1,0:T(1,128)} %cpl_hbm.1), custom_call_target="tpu_custom_call" | custom-call | flops 805306368 | bytes 1310720 | tf_op jit(solution)/shard_map/pallas_call | solution.py:235
  33.1 0.8 %copy.7 = f32[7,7,8,256]{3,2,1,0:T(8,128)} copy(f32[7,7,8,256]{3,2,1,0:T(8,128)S(1)} %shard_map.55) | data formatting | bytes 802816
